TPU v7x, 32 devices: a whole 2x2x4 slice. The times are simulated.
32 devices in a mesh: tiles: 8 (over y, x, core), reps: 4 (over z).
Axes of the slice: x: 2, y: 2, z: 4, core: 2. Of those that a mesh axis runs over, the one named last changes fastest.
Arguments:
- tiles_w: bfloat16 [1024, 128, 128], P('tiles'), may hold values from 0.0001 to 4
- tile_worker: int32 [1024], P('tiles'), may hold values from 0 to 15
- tile_owner: int32 [1024], P('tiles'), may hold values from 0 to 7
- owner_block: int32 [8, 8], P('tiles'), may hold values from 0 to 1
- worker_base: float32 [16384], P('tiles'), may hold values from -6 to 6
- worker_noise: float32 [16384], P('tiles'), may hold values from 0.2 to 1.5
- worker_cluster: int32 [16384], P('tiles'), may hold values from 0 to 255
- firm_base: float32 [2048], P('tiles'), may hold values from -6 to 6
- firm_noise: float32 [2048], P('tiles'), may hold values from 0.2 to 1.5
- firm_cluster: int32 [2048], P('tiles'), may hold values from 0 to 255
- signs: int32 [256, 256], P('reps'), may hold values from 0 to 1
- covariates: float32 [2048, 512], P('tiles'), may hold values from -0.125 to 0.125
- whitening: float32 [512, 512], replicated, may hold values from -0.25 to 0.25
Outputs:
- worker_effect: float32 [256, 16384], P('reps', 'tiles')
- firm_effect: float32 [256, 2048], P('reps', 'tiles')
- coefficients: float32 [256, 512], P('reps')
- covariance: float32 [512, 512], P('tiles')
Inputs may be any that keep to these rules, and one draw needn't show every extreme that they name: `tile_worker`: local worker block of each tile. `tile_owner`: owner of each tile's firm block. `owner_block`: firm block among the owner's 2 blocks. `signs`: a bit that gives the sign 2 b - 1.
All inputs are finite; a program needn't handle non-finite values.
Results may differ from a plain program's by a relative error of at most 0.0023.
Values may be sent and summed in bfloat16 or wider, within the bound.
A program may use at most 64 MiB of HBM per device.

v0:
```python
import functools

import jax
import jax.numpy as jnp
from jax import lax
from jax.experimental import pallas as pl
from jax.experimental.pallas import tpu as pltpu
from jax.sharding import PartitionSpec as P

SWEEPS = 6
WORK_BLOCKS = 16
spectral_bound = 0.8
F32, BF16 = jnp.float32, jnp.bfloat16
NN = (((1,), (0,)), ((), ()))
NT = (((1,), (1,)), ((), ()))
VMEM_BYTES = 60 * 2**20


def chebyshev_weights(sweep_count):
    weights = [1.0]
    weights.append(1.0 / (1.0 - 0.5 * spectral_bound * spectral_bound))
    while len(weights) < sweep_count:
        weights.append(1.0 / (1.0 - 0.25 * spectral_bound * spectral_bound * weights[-1]))
    return weights


def product(a, b, dims=NN):
    return lax.dot_general(a, b, dims, preferred_element_type=F32)


def split(a):
    high = a.astype(BF16)
    return high, (a - high.astype(F32)).astype(BF16)


def fine_product(a, b, dims=NN):
    ah, al = split(a)
    bh, bl = split(b)
    return product(ah, bh, dims) + (product(ah, bl, dims) + product(al, bh, dims))


def dense_kernel(worker_ref, owner_ref, tiles_ref, dense_ref, acc):
    tile_count, cells, _ = tiles_ref.shape
    acc[...] = jnp.zeros_like(acc)

    def add(t, _):
        rows = pl.ds(pl.multiple_of(worker_ref[t] * cells, cells), cells)
        o = owner_ref[t]
        acc[o, rows, :] += tiles_ref[t].astype(F32)
        return 0

    lax.fori_loop(0, tile_count, add, 0)
    for o in range(acc.shape[0]):
        dense_ref[o // 2, :, (o % 2) * cells : (o % 2 + 1) * cells] = acc[o].astype(BF16)


def dense_weights(tiles_w, tile_worker, tile_owner, n):
    cells = tiles_w.shape[1]
    workers = WORK_BLOCKS * cells
    return pl.pallas_call(
        dense_kernel,
        out_shape=jax.ShapeDtypeStruct((n // 2, workers, 2 * cells), BF16),
        in_specs=[
            pl.BlockSpec(memory_space=pltpu.SMEM),
            pl.BlockSpec(memory_space=pltpu.SMEM),
            pl.BlockSpec(memory_space=pltpu.VMEM),
        ],
        out_specs=pl.BlockSpec(memory_space=pltpu.VMEM),
        scratch_shapes=[pltpu.VMEM((n, workers, cells), F32)],
        compiler_params=pltpu.CompilerParams(vmem_limit_bytes=VMEM_BYTES),
    )(tile_worker, tile_owner, tiles_w)


def main_kernel(
    n,
    nz,
    blocks_ref,
    dense_ref,
    wbase_ref,
    wnoise_ref,
    wcluster_ref,
    fbase_ref,
    fnoise_ref,
    fcluster_ref,
    signs_ref,
    cov_ref,
    whit_ref,
    worker_ref,
    firm_ref,
    coef_ref,
    moment_ref,
    outcome,
    wscale,
    foutcome,
    fscale,
    older,
    newer,
    worker_bf,
    pull_sum,
    mixing,
    meta_s,
    meta_r,
    push_s,
    push_r,
    ret_s,
    ret_r,
    part_s,
    part_r,
    sum_s,
    sum_r,
    full,
    mom_s,
    mom_r,
    momsum_s,
    momsum_r,
    sems,
    zsems,
):
    me = lax.axis_index("tiles")
    mz = lax.axis_index("reps")
    chips = n // 2
    chip, core = me // 2, lax.rem(me, 2)
    reps = signs_ref.shape[0]
    cells = push_s.shape[2]
    firm_blocks = foutcome.shape[0]
    barrier = pltpu.get_barrier_semaphore()
    for k in range(1, n):
        pl.semaphore_signal(barrier, inc=1, device_id={"tiles": lax.rem(me + k, n)}, device_id_type=pl.DeviceIdType.MESH)
    for k in range(1, nz):
        pl.semaphore_signal(barrier, inc=1, device_id={"reps": lax.rem(mz + k, nz)}, device_id_type=pl.DeviceIdType.MESH)
    pl.semaphore_wait(barrier, n - 1 + nz - 1)

    def copy(source, target, kind, p):
        return pltpu.make_async_remote_copy(
            src_ref=source.at[p],
            dst_ref=target.at[me],
            send_sem=sems.at[kind, p],
            recv_sem=sems.at[kind + 1, me],
            device_id={"tiles": p},
            device_id_type=pl.DeviceIdType.MESH,
        )

    def finish(source, target, kind, p):
        got = pltpu.make_async_remote_copy(
            src_ref=source.at[p],
            dst_ref=target.at[p],
            send_sem=sems.at[kind, p],
            recv_sem=sems.at[kind + 1, p],
            device_id={"tiles": p},
            device_id_type=pl.DeviceIdType.MESH,
        )
        got.wait_send()
        got.wait_recv()

    def zcopy(source, target, kind, p, at):
        return pltpu.make_async_remote_copy(
            src_ref=source.at[p],
            dst_ref=target.at[at],
            send_sem=zsems.at[kind, p],
            recv_sem=zsems.at[kind + 1, at],
            device_id={"reps": p},
            device_id_type=pl.DeviceIdType.MESH,
        )

    def all_start(source, target, kind):
        for k in range(1, n):
            copy(source, target, kind, lax.rem(me + k, n)).start()

    def all_finish(source, target, kind):
        for k in range(1, n):
            finish(source, target, kind, lax.rem(me + k, n))

    def chip_order(first):
        return [lax.rem(chip + k, chips) for k in (range(chips) if first else list(range(1, chips)) + [0])]

    row = lax.broadcasted_iota(jnp.int32, (8, cells), 0)
    ones_col = jnp.ones((8, dense_ref.shape[1]), BF16)
    for c in range(chips):
        mass = product(ones_col, dense_ref[c])
        for h in range(2):
            o = 2 * c + h
            block = blocks_ref[0:1, o : o + 1].astype(F32)
            meta_s[o] = jnp.where(row == 0, mass[:, h * cells : (h + 1) * cells], block)
    meta_r[me] = meta_s[me]
    all_start(meta_s, meta_r, 0)

    flips = (2 * signs_ref[...] - 1).astype(BF16)

    def wild(base, noise, cluster):
        ids = lax.broadcasted_iota(jnp.int32, (flips.shape[1], cluster.shape[1]), 0)
        hot = jnp.where(ids == cluster, 1.0, 0.0).astype(BF16)
        return base + noise * product(flips, hot)

    step = min(512, wbase_ref.shape[1])
    for at in range(0, wbase_ref.shape[1], step):
        cols = slice(at, at + step)
        value = wild(wbase_ref[:, cols], wnoise_ref[:, cols], wcluster_ref[:, cols])
        outcome[:, cols] = value
        worker_bf[:, cols] = value.astype(BF16)

    def push():
        for c in chip_order(False):
            part = product(worker_bf[...], dense_ref[c]).astype(BF16)
            for h in range(2):
                push_s[2 * c + h] = part[:, h * cells : (h + 1) * cells]

            for h in range(2):
                p = 2 * c + h

                @pl.when(p != me)
                def _():
                    copy(push_s, push_r, 2, p).start()

        push_r[me] = push_s[me]

    push()
    for b in range(firm_blocks):
        cols = slice(b * cells, (b + 1) * cells)
        foutcome[b] = wild(fbase_ref[:, cols], fnoise_ref[:, cols], fcluster_ref[:, cols])
    older[...] = jnp.zeros_like(older)
    newer[...] = jnp.zeros_like(newer)
    ones_row = jnp.ones((8, 2 * cells), BF16)
    degree = product(ones_row, dense_ref[0], NT)
    for c in range(1, chips):
        degree += product(ones_row, dense_ref[c], NT)
    wscale[...] = 1.0 / (1.0 + degree)
    mixing[...] = fine_product(cov_ref[...], whit_ref[...], NT)
    all_finish(meta_s, meta_r, 0)
    for b in range(firm_blocks):
        total = jnp.ones((1, cells), F32)
        for s in range(n):
            total += jnp.where(meta_r[s, 1:2, :] == float(b), meta_r[s, 0:1, :], 0.0)
        fscale[b] = jnp.broadcast_to(1.0 / total, (8, cells))

    def take_push(omega):
        all_finish(push_s, push_r, 2)
        sums = [jnp.zeros((reps, cells), F32) for _ in range(firm_blocks)]
        for s in range(n):
            value = push_r[s].astype(F32)
            block = meta_r[s, 1:2, :]
            for b in range(firm_blocks):
                sums[b] += jnp.where(block == float(b), value, 0.0)
        for b in range(firm_blocks):
            target = foutcome[b] - sums[b] * fscale[b, 0:1, :]
            old = older[b]
            older[b] = newer[b]
            newer[b] = old + omega * (target - old)

    omegas = chebyshev_weights(SWEEPS)

    def sweep(k, _):
        omega = jnp.float32(omegas[0])
        for i in range(1, SWEEPS - 1):
            omega = jnp.where(k == i, jnp.float32(omegas[i]), omega)
        take_push(omega)
        firm = [newer[b] for b in range(firm_blocks)]
        for d in range(1, n + 1):
            p = lax.rem(me + d, n)
            value = firm[0]
            for b in range(1, firm_blocks):
                value = jnp.where(meta_r[p, 1:2, :] == float(b), firm[b], value)
            ret_s[p] = value.astype(BF16)
            if d < n:
                copy(ret_s, ret_r, 4, p).start()
        ret_r[me] = ret_s[me]
        for i, c in enumerate(chip_order(True)):
            for h in range(2):
                p = 2 * c + h

                @pl.when(p != me)
                def _():
                    finish(ret_s, ret_r, 4, p)

            pair = jnp.concatenate([ret_r[2 * c], ret_r[2 * c + 1]], axis=1)
            part = product(pair, dense_ref[c], NT)
            if i == 0:
                pull_sum[...] = part
            else:
                pull_sum[...] += part
        value = outcome[...] - pull_sum[...] * wscale[0:1, :]
        worker_ref[...] = value
        worker_bf[...] = value.astype(BF16)
        push()
        return 0

    lax.fori_loop(0, SWEEPS - 1, sweep, 0)
    take_push(jnp.float32(omegas[SWEEPS - 1]))
    for b in range(firm_blocks):
        firm_ref[:, b * cells : (b + 1) * cells] = newer[b]

    term = fine_product(firm_ref[...], mixing[...])
    share = reps // n
    for p in range(n):
        part_s[p] = term[p * share : (p + 1) * share, :]
    part_r[me] = part_s[me]
    all_start(part_s, part_r, 6)
    all_finish(part_s, part_r, 6)
    total = part_r[0]
    for p in range(1, n):
        total += part_r[p]
    for p in range(n):
        sum_s[p] = total
    sum_r[me] = total
    all_start(sum_s, sum_r, 8)
    all_finish(sum_s, sum_r, 8)
    for p in range(n):
        coef_ref[p * share : (p + 1) * share, :] = sum_r[p]

    coef = coef_ref[...]
    whole = fine_product(coef.T, coef)
    piece = full.shape[1]
    for i in range(n * nz):
        full[i] = whole[i * piece : (i + 1) * piece, :]
    for z in range(nz):
        mom_s[z] = full[me * nz + z]
    mom_r[mz] = mom_s[mz]
    for k in range(1, nz):
        zcopy(mom_s, mom_r, 0, lax.rem(mz + k, nz), mz).start()
    for k in range(1, nz):
        p = lax.rem(mz + k, nz)
        got = zcopy(mom_s, mom_r, 0, p, p)
        got.wait_send()
        got.wait_recv()
    total = mom_r[0]
    for z in range(1, nz):
        total += mom_r[z]
    total = total * (1.0 / (reps * nz))
    for z in range(nz):
        momsum_s[z] = total
    momsum_r[mz] = total
    for k in range(1, nz):
        zcopy(momsum_s, momsum_r, 2, lax.rem(mz + k, nz), mz).start()
    for k in range(1, nz):
        p = lax.rem(mz + k, nz)
        got = zcopy(momsum_s, momsum_r, 2, p, p)
        got.wait_send()
        got.wait_recv()
    for z in range(nz):
        moment_ref[z * piece : (z + 1) * piece, :] = momsum_r[z]


def body(
    tiles_w,
    tile_worker,
    tile_owner,
    owner_block,
    worker_base,
    worker_noise,
    worker_cluster,
    firm_base,
    firm_noise,
    firm_cluster,
    signs,
    covariates,
    whitening,
):
    n, nz = lax.axis_size("tiles"), lax.axis_size("reps")
    cells = tiles_w.shape[1]
    reps = signs.shape[0]
    workers, firms = worker_base.shape[0], firm_base.shape[0]
    blocks = firms // cells
    covars = covariates.shape[1]
    dense = dense_weights(tiles_w, tile_worker, tile_owner, n)
    own = covars // n
    vm = pltpu.VMEM
    return pl.pallas_call(
        functools.partial(main_kernel, n, nz),
        out_shape=(
            jax.ShapeDtypeStruct((reps, workers), F32),
            jax.ShapeDtypeStruct((reps, firms), F32),
            jax.ShapeDtypeStruct((reps, covars), F32),
            jax.ShapeDtypeStruct((own, covars), F32),
        ),
        in_specs=[pl.BlockSpec(memory_space=vm)] * 11,
        out_specs=[pl.BlockSpec(memory_space=vm)] * 4,
        scratch_shapes=[
            vm((reps, workers), F32),
            vm((8, workers), F32),
            vm((blocks, reps, cells), F32),
            vm((blocks, 8, cells), F32),
            vm((blocks, reps, cells), F32),
            vm((blocks, reps, cells), F32),
            vm((reps, workers), BF16),
            vm((reps, workers), F32),
            vm((firms, covars), F32),
            vm((n, 8, cells), F32),
            vm((n, 8, cells), F32),
            vm((n, reps, cells), BF16),
            vm((n, reps, cells), BF16),
            vm((n, reps, cells), BF16),
            vm((n, reps, cells), BF16),
            vm((n, reps // n, covars), F32),
            vm((n, reps // n, covars), F32),
            vm((n, reps // n, covars), F32),
            vm((n, reps // n, covars), F32),
            vm((n * nz, own // nz, covars), F32),
            vm((nz, own // nz, covars), F32),
            vm((nz, own // nz, covars), F32),
            vm((nz, own // nz, covars), F32),
            vm((nz, own // nz, covars), F32),
            pltpu.SemaphoreType.DMA((10, n)),
            pltpu.SemaphoreType.DMA((4, nz)),
        ],
        compiler_params=pltpu.CompilerParams(
            collective_id=0, has_side_effects=True, vmem_limit_bytes=VMEM_BYTES
        ),
    )(
        owner_block,
        dense,
        worker_base[None],
        worker_noise[None],
        worker_cluster[None],
        firm_base[None],
        firm_noise[None],
        firm_cluster[None],
        signs,
        covariates,
        whitening,
    )


def solution(mesh):
    t = P("tiles")
    rows = P("tiles", None)
    placed = (P("tiles", None, None), t, t, rows, t, t, t, t, t, t, P("reps", None), rows, P())
    return jax.shard_map(
        body,
        mesh=mesh,
        in_specs=placed,
        out_specs=(P("reps", "tiles"), P("reps", "tiles"), P("reps", None), P("tiles", None)),
        check_vma=False,
    )
```

profile of v0, /device:TPU:0, one launch (start us, length us, event | category | flops | bytes accessed | tf_op | source)
XLA Modules:
  0.0 89.6 jit_solution(12419356070101525732)
XLA Ops:
  0.6 6.7 %shard_map.156.dense_ref = bf16[4,2048,256]{2,1,0:T(8,128)(2,1)} custom-call(s32[128]{0:T(128)} %worker_ref.1, s32[128]{0:T(128)} %owner_ref.1, bf16[128,128,128]{2,1,0:T(8,128)(2,1)} %tiles_ref.1), custom_call_target="tpu_custom_call" | custom-call | tf_op jit(solution)/shard_map/pallas_call | solution.py:60
  7.3 75.8 %shard_map.157 = (f32[64,2048]{1,0:T(8,128)}, f32[64,256]{1,0:T(8,128)}, f32[64,512]{1,0:T(8,128)}, f32[64,512]{1,0:T(8,128)}) custom-call(s32[1,8]{1,0:T(1,128)} %blocks_ref.1, bf16[4,2048,256]{2,1,0:T(8,128)(2,1)} %shard_map.156.dense_ref, f32[1,2048]{1,0:T(1,128)} %bitcast.6, f32[1,2048]{1,0:T(1,128)} %bitcast.7, s32[1,2048]{1,0:T(1,128)} %bitcast.8, ...), custom_call_target="tpu_custom_call" | custom-call | tf_op jit(solution)/shard_map/pallas_call | solution.py:366
  83.1 1.9 %copy.21 = f32[64,2048]{1,0:T(8,128)} copy(f32[64,2048]{1,0:T(8,128)} %get-tuple-element.8) | data formatting | bytes 1048576
  85.0 1.5 %copy.22 = f32[64,256]{1,0:T(8,128)} copy(f32[64,256]{1,0:T(8,128)} %get-tuple-element.9) | data formatting | bytes 131072
  86.5 1.6 %copy.23 = f32[64,512]{1,0:T(8,128)} copy(f32[64,512]{1,0:T(8,128)} %get-tuple-element.10) | data formatting | bytes 262144
  88.0 1.6 %copy.24 = f32[64,512]{1,0:T(8,128)} copy(f32[64,512]{1,0:T(8,128)} %get-tuple-element.11) | data formatting | bytes 262144
where the time goes:
time: 89.9 us; the launch traced here: 89.6 us
  Pallas kernels  82.5 us (92%)
  local copies, waits for them, and re-layouts  6.48 us (7%)
    pallas_call x1, Pallas kernels, body(): pl.pallas_call(functools.partial(main_kernel, n, nz), out_shape=(jax.Shap...  75.8 us
    pallas_call x1, Pallas kernels, dense_weights(): pl.pallas_call(dense_kernel, out_shape=jax.ShapeDtypeStruct((n // 2, work...  6.7 us
    unnamed x4, local copies, waits for them, and re-layouts  6.48 us

commit v1 on v0

--- a/solution.py
+++ b/solution.py
@@ -49,7 +49,7 @@
         acc[o, rows, :] += tiles_ref[t].astype(F32)
         return 0
 
-    lax.fori_loop(0, tile_count, add, 0)
+    lax.fori_loop(0, tile_count, add, 0, unroll=8)
     for o in range(acc.shape[0]):
         dense_ref[o // 2, :, (o % 2) * cells : (o % 2 + 1) * cells] = acc[o].astype(BF16)
 
@@ -67,7 +67,9 @@
         ],
         out_specs=pl.BlockSpec(memory_space=pltpu.VMEM),
         scratch_shapes=[pltpu.VMEM((n, workers, cells), F32)],
-        compiler_params=pltpu.CompilerParams(vmem_limit_bytes=VMEM_BYTES),
+        compiler_params=pltpu.CompilerParams(
+            vmem_limit_bytes=min(VMEM_BYTES, n * workers * cells * 6 + tiles_w.size * 2 + 4 * 2**20)
+        ),
     )(tile_worker, tile_owner, tiles_w)
 
 
@@ -128,7 +130,6 @@
         pl.semaphore_signal(barrier, inc=1, device_id={"tiles": lax.rem(me + k, n)}, device_id_type=pl.DeviceIdType.MESH)
     for k in range(1, nz):
         pl.semaphore_signal(barrier, inc=1, device_id={"reps": lax.rem(mz + k, nz)}, device_id_type=pl.DeviceIdType.MESH)
-    pl.semaphore_wait(barrier, n - 1 + nz - 1)
 
     def copy(source, target, kind, p):
         return pltpu.make_async_remote_copy(
@@ -149,8 +150,7 @@
             device_id={"tiles": p},
             device_id_type=pl.DeviceIdType.MESH,
         )
-        got.wait_send()
-        got.wait_recv()
+        return got
 
     def zcopy(source, target, kind, p, at):
         return pltpu.make_async_remote_copy(
@@ -163,15 +163,33 @@
         )
 
     def all_start(source, target, kind):
-        for k in range(1, n):
-            copy(source, target, kind, lax.rem(me + k, n)).start()
+        for p in partners(False):
+            copy(source, target, kind, p).start()
 
     def all_finish(source, target, kind):
-        for k in range(1, n):
-            finish(source, target, kind, lax.rem(me + k, n))
+        for p in partners(True):
+            finish(source, target, kind, p).wait_recv()
+        all_sent(source, target, kind)
+
+    def all_sent(source, target, kind):
+        for p in partners(False):
+            finish(source, target, kind, p).wait_send()
+
+    def mate(k):
+        if chips & (chips - 1):
+            return lax.rem(chip + k, chips)
+        other = 0
+        for b in (1 << e for e in range(chips.bit_length() - 1)):
+            bit = lax.rem(chip // b, 2)
+            other = other + b * (1 - bit if k & b else bit)
+        return other
 
     def chip_order(first):
-        return [lax.rem(chip + k, chips) for k in (range(chips) if first else list(range(1, chips)) + [0])]
+        return [mate(k) for k in (range(chips) if first else range(chips - 1, -1, -1))]
+
+    def partners(near):
+        order = [2 * mate(k) + lax.rem(core + h, 2) for k in range(chips) for h in range(2)][1:]
+        return order if near else order[::-1]
 
     row = lax.broadcasted_iota(jnp.int32, (8, cells), 0)
     ones_col = jnp.ones((8, dense_ref.shape[1]), BF16)
@@ -181,8 +199,6 @@
             o = 2 * c + h
             block = blocks_ref[0:1, o : o + 1].astype(F32)
             meta_s[o] = jnp.where(row == 0, mass[:, h * cells : (h + 1) * cells], block)
-    meta_r[me] = meta_s[me]
-    all_start(meta_s, meta_r, 0)
 
     flips = (2 * signs_ref[...] - 1).astype(BF16)
 
@@ -197,6 +213,10 @@
         value = wild(wbase_ref[:, cols], wnoise_ref[:, cols], wcluster_ref[:, cols])
         outcome[:, cols] = value
         worker_bf[:, cols] = value.astype(BF16)
+
+    pl.semaphore_wait(barrier, n - 1 + nz - 1)
+    meta_r[me] = meta_s[me]
+    all_start(meta_s, meta_r, 0)
 
     def push():
         for c in chip_order(False):
@@ -233,9 +253,10 @@
         fscale[b] = jnp.broadcast_to(1.0 / total, (8, cells))
 
     def take_push(omega):
-        all_finish(push_s, push_r, 2)
         sums = [jnp.zeros((reps, cells), F32) for _ in range(firm_blocks)]
-        for s in range(n):
+        for s in [me] + partners(True):
+            if s is not me:
+                finish(push_s, push_r, 2, s).wait_recv()
             value = push_r[s].astype(F32)
             block = meta_r[s, 1:2, :]
             for b in range(firm_blocks):
@@ -254,22 +275,22 @@
             omega = jnp.where(k == i, jnp.float32(omegas[i]), omega)
         take_push(omega)
         firm = [newer[b] for b in range(firm_blocks)]
-        for d in range(1, n + 1):
-            p = lax.rem(me + d, n)
+        for p in partners(False) + [me]:
             value = firm[0]
             for b in range(1, firm_blocks):
                 value = jnp.where(meta_r[p, 1:2, :] == float(b), firm[b], value)
             ret_s[p] = value.astype(BF16)
-            if d < n:
+            if p is not me:
                 copy(ret_s, ret_r, 4, p).start()
         ret_r[me] = ret_s[me]
+        all_sent(push_s, push_r, 2)
         for i, c in enumerate(chip_order(True)):
             for h in range(2):
                 p = 2 * c + h
 
                 @pl.when(p != me)
                 def _():
-                    finish(ret_s, ret_r, 4, p)
+                    finish(ret_s, ret_r, 4, p).wait_recv()
 
             pair = jnp.concatenate([ret_r[2 * c], ret_r[2 * c + 1]], axis=1)
             part = product(pair, dense_ref[c], NT)
@@ -281,10 +302,12 @@
         worker_ref[...] = value
         worker_bf[...] = value.astype(BF16)
         push()
+        all_sent(ret_s, ret_r, 4)
         return 0
 
     lax.fori_loop(0, SWEEPS - 1, sweep, 0)
     take_push(jnp.float32(omegas[SWEEPS - 1]))
+    all_sent(push_s, push_r, 2)
     for b in range(firm_blocks):
         firm_ref[:, b * cells : (b + 1) * cells] = newer[b]
 
@@ -339,6 +362,27 @@
         moment_ref[z * piece : (z + 1) * piece, :] = momsum_r[z]
 
 
+def emit_kernel(*refs):
+    sems = refs[-1]
+    half = len(refs) // 2
+    copies = [pltpu.make_async_copy(refs[i], refs[half + i], sems.at[i]) for i in range(half)]
+    for c in copies:
+        c.start()
+    for c in copies:
+        c.wait()
+
+
+def emit(results):
+    return pl.pallas_call(
+        emit_kernel,
+        out_shape=tuple(jax.ShapeDtypeStruct(r.shape, r.dtype) for r in results),
+        in_specs=[pl.BlockSpec(memory_space=pl.ANY)] * len(results),
+        out_specs=[pl.BlockSpec(memory_space=pl.ANY)] * len(results),
+        scratch_shapes=[pltpu.SemaphoreType.DMA((len(results),))],
+        compiler_params=pltpu.CompilerParams(vmem_limit_bytes=2**20),
+    )(*results)
+
+
 def body(
     tiles_w,
     tile_worker,
@@ -363,7 +407,7 @@
     dense = dense_weights(tiles_w, tile_worker, tile_owner, n)
     own = covars // n
     vm = pltpu.VMEM
-    return pl.pallas_call(
+    results = pl.pallas_call(
         functools.partial(main_kernel, n, nz),
         out_shape=(
             jax.ShapeDtypeStruct((reps, workers), F32),
@@ -402,7 +446,7 @@
             pltpu.SemaphoreType.DMA((4, nz)),
         ],
         compiler_params=pltpu.CompilerParams(
-            collective_id=0, has_side_effects=True, vmem_limit_bytes=VMEM_BYTES
+            collective_id=0, has_side_effects=True, vmem_limit_bytes=dense.size * 2 + 20 * 2**20
         ),
     )(
         owner_block,
@@ -417,6 +461,7 @@
         covariates,
         whitening,
     )
+    return emit(results)
 
 
 def solution(mesh):

time: 89.9 us -> 77.7 us (0.86)
  Pallas kernels: 82.5 us -> 73.2 us
  local copies, waits for them, and re-layouts: 6.48 us -> 3.53 us
    pallas_call x1, Pallas kernels: 75.8 us -> 69.6 us  [body(): pl.pallas_call(functools.partial(main_kernel, n, nz), out_shape=(jax.Shap...]
    pallas_call x1, Pallas kernels: 6.7 us -> 2.67 us  [dense_weights(): pl.pallas_call(dense_kernel, out_shape=jax.ShapeDtypeStruct((n // 2, work...]
    unnamed x4 -> x26, local copies, waits for them, and re-layouts: 6.48 us -> 3.53 us
    pallas_call x0 -> x1, Pallas kernels: none -> 0.93 us  [emit(): pl.pallas_call(emit_kernel, out_shape=tuple((jax.ShapeDtypeStruct(r.shape...]
where the time goes in v1:
time: 77.7 us; the launch traced here: 77.5 us
  Pallas kernels  73.2 us (94%)
  local copies, waits for them, and re-layouts  3.53 us (5%)
  between operations  0.79 us (1%)
    pallas_call x1, Pallas kernels, body(): pl.pallas_call(functools.partial(main_kernel, n, nz), out_shape=(jax.Shap...  69.6 us
    unnamed x26, local copies, waits for them, and re-layouts  3.53 us
    pallas_call x1, Pallas kernels, dense_weights(): pl.pallas_call(dense_kernel, out_shape=jax.ShapeDtypeStruct((n // 2, work...  2.67 us

profile of v1, /device:TPU:0, one launch (start us, length us, event | category | flops | bytes accessed | tf_op | source)
XLA Modules:
  0.0 77.5 jit_solution(644372137695964121)
XLA Ops:
  0.6 0.0 copy-start
  0.6 2.2 %copy-done = bf16[128,128,128]{2,1,0:T(8,128)(2,1)S(1)} copy-done((bf16[128,128,128]{2,1,0:T(8,128)(2,1)S(1)}, bf16[128,128,128]{2,1,0:T(8,128)(2,1)}, u32[]{:S(2)}) %copy-start) | copy-done | bytes 4194328
  2.8 0.0 copy-start.10
  2.8 0.7 copy-done.10
  3.5 0.7 copy-done.11
  4.1 0.0 copy-start.5
  4.2 0.0 copy-start.6
  4.2 0.0 copy-start.7
  4.2 0.0 copy-start.8
  4.2 0.0 copy-start.9
  4.2 0.0 copy-start.12
  4.2 2.7 %shard_map.156.dense_ref = bf16[4,2048,256]{2,1,0:T(8,128)(2,1)S(1)} custom-call(s32[128]{0:T(128)S(1)} %copy-done.10, s32[128]{0:T(128)S(1)} %copy-done.11, bf16[128,128,128]{2,1,0:T(8,128)(2,1)S(1)} %copy-done), custom_call_target="tpu_custom_call" | custom-call | tf_op jit(solution)/shard_map/pallas_call | solution.py:60
  6.9 0.0 copy-done.1
  6.9 0.0 copy-done.2
  6.9 0.0 copy-done.3
  6.9 0.0 copy-done.4
  6.9 0.0 copy-done.5
  6.9 0.0 copy-done.6
  6.9 0.0 copy-done.7
  7.0 0.0 copy-done.8
  7.0 0.0 copy-done.9
  7.0 0.0 copy-done.12
  7.0 69.6 %shard_map.157 = (f32[64,2048]{1,0:T(8,128)S(1)}, f32[64,256]{1,0:T(8,128)S(1)}, f32[64,512]{1,0:T(8,128)S(1)}, f32[64,512]{1,0:T(8,128)S(1)}) custom-call(s32[1,8]{1,0:T(1,128)S(1)} %copy-done.12, bf16[4,2048,256]{2,1,0:T(8,128)(2,1)S(1)} %shard_map.156.dense_ref, f32[1,2048]{1,0:T(1,128)S(1)} %bitcast.6, f32[1,2048]{1,0:T(1,128)S(1)} %bitcast.7, ...), custom_call_target="tpu_custom_call" | custom-call | tf_op jit(solution)/shard_map/pallas_call | solution.py:410
  76.6 0.9 %shard_map.158 = (f32[64,2048]{1,0:T(8,128)}, f32[64,256]{1,0:T(8,128)}, f32[64,512]{1,0:T(8,128)}, f32[64,512]{1,0:T(8,128)}) custom-call(f32[64,2048]{1,0:T(8,128)S(1)} %get-tuple-element.8.refs_0_, f32[64,256]{1,0:T(8,128)S(1)} %get-tuple-element.9.refs_1_, f32[64,512]{1,0:T(8,128)S(1)} %get-tuple-element.10.refs_2_, f32[64,512]{1,0:T(8,128)S(1)} %get-tuple-element.11.refs_3_), custom_call_target="tpu_custom_call" | custom-call | tf_op jit(solution)/shard_map/pallas_call | solution.py:376
  (5 shorter events, 0.0 us)
Async XLA Ops:
  0.6 2.2 %copy-start = (bf16[128,128,128]{2,1,0:T(8,128)(2,1)S(1)}, bf16[128,128,128]{2,1,0:T(8,128)(2,1)}, u32[]{:S(2)}) copy-start(bf16[128,128,128]{2,1,0:T(8,128)(2,1)} %tiles_ref.1) | copy-start | bytes 12582916
  2.8 0.7 copy-start.10
  3.5 0.7 copy-start.11
  4.1 2.8 %copy-start.1 = (f32[512,512]{1,0:T(8,128)S(1)}, f32[512,512]{1,0:T(8,128)}, u32[]{:S(2)}) copy-start(f32[512,512]{1,0:T(8,128)} %whit_ref.1) | copy-start | bytes 3145732
  4.1 2.8 %copy-start.2 = (f32[256,512]{1,0:T(8,128)S(1)}, f32[256,512]{1,0:T(8,128)}, u32[]{:S(2)}) copy-start(f32[256,512]{1,0:T(8,128)} %cov_ref.1) | copy-start | bytes 1572868
  4.1 2.8 %copy-start.3 = (s32[64,256]{1,0:T(8,128)S(1)}, s32[64,256]{1,0:T(8,128)}, u32[]{:S(2)}) copy-start(s32[64,256]{1,0:T(8,128)} %signs_ref.1) | copy-start | bytes 196612
  4.1 2.8 %copy-start.4 = (f32[2048]{0:T(1024)S(1)}, f32[2048]{0:T(1024)}, u32[]{:S(2)}) copy-start(f32[2048]{0:T(1024)} %param.17) | copy-start | bytes 24580
  4.1 2.8 %copy-start.5 = (f32[2048]{0:T(1024)S(1)}, f32[2048]{0:T(1024)}, u32[]{:S(2)}) copy-start(f32[2048]{0:T(1024)} %param.18) | copy-start | bytes 24580
  4.2 2.8 %copy-start.6 = (s32[2048]{0:T(1024)S(1)}, s32[2048]{0:T(1024)}, u32[]{:S(2)}) copy-start(s32[2048]{0:T(1024)} %param.19) | copy-start | bytes 24580
  4.2 2.8 %copy-start.7 = (f32[256]{0:T(256)S(1)}, f32[256]{0:T(256)}, u32[]{:S(2)}) copy-start(f32[256]{0:T(256)} %param.20) | copy-start | bytes 3076
  4.2 2.8 %copy-start.8 = (f32[256]{0:T(256)S(1)}, f32[256]{0:T(256)}, u32[]{:S(2)}) copy-start(f32[256]{0:T(256)} %param.21) | copy-start | bytes 3076
  4.2 2.8 %copy-start.9 = (s32[256]{0:T(256)S(1)}, s32[256]{0:T(256)}, u32[]{:S(2)}) copy-start(s32[256]{0:T(256)} %param.22) | copy-start | bytes 3076
  4.2 2.8 %copy-start.12 = (s32[1,8]{1,0:T(1,128)S(1)}, s32[1,8]{1,0:T(1,128)}, u32[]{:S(2)}) copy-start(s32[1,8]{1,0:T(1,128)} %blocks_ref.1) | copy-start | bytes 100

commit v2 on v1

--- a/solution.py
+++ b/solution.py
@@ -111,10 +111,10 @@
     sum_s,
     sum_r,
     full,
-    mom_s,
-    mom_r,
-    momsum_s,
-    momsum_r,
+    zall,
+    other_s,
+    other_r,
+    allco,
     sems,
     zsems,
 ):
@@ -151,16 +151,6 @@
             device_id_type=pl.DeviceIdType.MESH,
         )
         return got
-
-    def zcopy(source, target, kind, p, at):
-        return pltpu.make_async_remote_copy(
-            src_ref=source.at[p],
-            dst_ref=target.at[at],
-            send_sem=zsems.at[kind, p],
-            recv_sem=zsems.at[kind + 1, at],
-            device_id={"reps": p},
-            device_id_type=pl.DeviceIdType.MESH,
-        )
 
     def all_start(source, target, kind):
         for p in partners(False):
@@ -321,45 +311,67 @@
     total = part_r[0]
     for p in range(1, n):
         total += part_r[p]
-    for p in range(n):
-        sum_s[p] = total
+    sum_s[...] = total
+    for k in range(1, nz):
+        pltpu.make_async_remote_copy(
+            src_ref=sum_s,
+            dst_ref=zall.at[mz],
+            send_sem=zsems.at[0, lax.rem(mz + k, nz)],
+            recv_sem=zsems.at[1, mz],
+            device_id={"reps": lax.rem(mz + k, nz)},
+            device_id_type=pl.DeviceIdType.MESH,
+        ).start()
     sum_r[me] = total
-    all_start(sum_s, sum_r, 8)
-    all_finish(sum_s, sum_r, 8)
+
+    def share_copy(kind, source, target, p, at):
+        return pltpu.make_async_remote_copy(
+            src_ref=source,
+            dst_ref=target.at[at],
+            send_sem=sems.at[kind, p],
+            recv_sem=sems.at[kind + 1, at],
+            device_id={"tiles": p},
+            device_id_type=pl.DeviceIdType.MESH,
+        )
+
+    for p in partners(False):
+        share_copy(8, sum_s, sum_r, p, me).start()
+    for k in range(1, nz):
+        p = lax.rem(mz + k, nz)
+        got = pltpu.make_async_remote_copy(
+            src_ref=sum_s,
+            dst_ref=zall.at[p],
+            send_sem=zsems.at[0, p],
+            recv_sem=zsems.at[1, p],
+            device_id={"reps": p},
+            device_id_type=pl.DeviceIdType.MESH,
+        )
+        got.wait_recv()
+        got.wait_send()
+        other_s[k - 1] = zall[p]
+    other_r[me] = other_s[...]
+    for p in partners(False):
+        share_copy(10, other_s, other_r, p, me).start()
+    for p in partners(True):
+        share_copy(8, sum_s, sum_r, p, p).wait_recv()
     for p in range(n):
         coef_ref[p * share : (p + 1) * share, :] = sum_r[p]
-
-    coef = coef_ref[...]
-    whole = fine_product(coef.T, coef)
+        allco[p * share : (p + 1) * share, :] = sum_r[p]
+    for p in partners(True):
+        share_copy(10, other_s, other_r, p, p).wait_recv()
+    for p in range(n):
+        for k in range(nz - 1):
+            at = reps + (p * (nz - 1) + k) * share
+            allco[at : at + share, :] = other_r[p, k]
+    for p in partners(True):
+        share_copy(8, sum_s, sum_r, p, p).wait_send()
+        share_copy(10, other_s, other_r, p, p).wait_send()
+
+    coef = allco[...]
+    whole = fine_product(coef.T, coef) * (1.0 / (reps * nz))
     piece = full.shape[1]
-    for i in range(n * nz):
+    for i in range(n):
         full[i] = whole[i * piece : (i + 1) * piece, :]
-    for z in range(nz):
-        mom_s[z] = full[me * nz + z]
-    mom_r[mz] = mom_s[mz]
-    for k in range(1, nz):
-        zcopy(mom_s, mom_r, 0, lax.rem(mz + k, nz), mz).start()
-    for k in range(1, nz):
-        p = lax.rem(mz + k, nz)
-        got = zcopy(mom_s, mom_r, 0, p, p)
-        got.wait_send()
-        got.wait_recv()
-    total = mom_r[0]
-    for z in range(1, nz):
-        total += mom_r[z]
-    total = total * (1.0 / (reps * nz))
-    for z in range(nz):
-        momsum_s[z] = total
-    momsum_r[mz] = total
-    for k in range(1, nz):
-        zcopy(momsum_s, momsum_r, 2, lax.rem(mz + k, nz), mz).start()
-    for k in range(1, nz):
-        p = lax.rem(mz + k, nz)
-        got = zcopy(momsum_s, momsum_r, 2, p, p)
-        got.wait_send()
-        got.wait_recv()
-    for z in range(nz):
-        moment_ref[z * piece : (z + 1) * piece, :] = momsum_r[z]
+    moment_ref[...] = full[me]
 
 
 def emit_kernel(*refs):
@@ -435,15 +447,15 @@
             vm((n, reps, cells), BF16),
             vm((n, reps // n, covars), F32),
             vm((n, reps // n, covars), F32),
+            vm((reps // n, covars), F32),
             vm((n, reps // n, covars), F32),
-            vm((n, reps // n, covars), F32),
-            vm((n * nz, own // nz, covars), F32),
-            vm((nz, own // nz, covars), F32),
-            vm((nz, own // nz, covars), F32),
-            vm((nz, own // nz, covars), F32),
-            vm((nz, own // nz, covars), F32),
-            pltpu.SemaphoreType.DMA((10, n)),
-            pltpu.SemaphoreType.DMA((4, nz)),
+            vm((n, own, covars), F32),
+            vm((nz, reps // n, covars), F32),
+            vm((nz - 1, reps // n, covars), F32),
+            vm((n, nz - 1, reps // n, covars), F32),
+            vm((reps * nz, covars), F32),
+            pltpu.SemaphoreType.DMA((12, n)),
+            pltpu.SemaphoreType.DMA((2, nz)),
         ],
         compiler_params=pltpu.CompilerParams(
             collective_id=0, has_side_effects=True, vmem_limit_bytes=dense.size * 2 + 20 * 2**20

time: 77.7 us -> 73.9 us (0.951)
  Pallas kernels: 73.2 us -> 69.4 us
    pallas_call x1, Pallas kernels: 69.6 us -> 65.8 us  [body(): pl.pallas_call(functools.partial(main_kernel, n, nz), out_shape=(jax.Shap...]
where the time goes in v2:
time: 73.9 us; the launch traced here: 73.7 us
  Pallas kernels  69.4 us (94%)
  local copies, waits for them, and re-layouts  3.53 us (5%)
  between operations  0.79 us (1%)
    pallas_call x1, Pallas kernels, body(): pl.pallas_call(functools.partial(main_kernel, n, nz), out_shape=(jax.Shap...  65.8 us
    unnamed x26, local copies, waits for them, and re-layouts  3.53 us
    pallas_call x1, Pallas kernels, dense_weights(): pl.pallas_call(dense_kernel, out_shape=jax.ShapeDtypeStruct((n // 2, work...  2.67 us

profile of v2, /device:TPU:0, one launch (start us, length us, event | category | flops | bytes accessed | tf_op | source)
XLA Modules:
  0.0 73.7 jit_solution(12960760137941189952)
XLA Ops:
  0.6 0.0 copy-start
  0.6 2.2 %copy-done = bf16[128,128,128]{2,1,0:T(8,128)(2,1)S(1)} copy-done((bf16[128,128,128]{2,1,0:T(8,128)(2,1)S(1)}, bf16[128,128,128]{2,1,0:T(8,128)(2,1)}, u32[]{:S(2)}) %copy-start) | copy-done | bytes 4194328
  2.8 0.0 copy-start.10
  2.8 0.7 copy-done.10
  3.5 0.7 copy-done.11
  4.1 0.0 copy-start.5
  4.2 0.0 copy-start.6
  4.2 0.0 copy-start.7
  4.2 0.0 copy-start.8
  4.2 0.0 copy-start.9
  4.2 0.0 copy-start.12
  4.2 2.7 %shard_map.156.dense_ref = bf16[4,2048,256]{2,1,0:T(8,128)(2,1)S(1)} custom-call(s32[128]{0:T(128)S(1)} %copy-done.10, s32[128]{0:T(128)S(1)} %copy-done.11, bf16[128,128,128]{2,1,0:T(8,128)(2,1)S(1)} %copy-done), custom_call_target="tpu_custom_call" | custom-call | tf_op jit(solution)/shard_map/pallas_call | solution.py:60
  6.9 0.0 copy-done.1
  6.9 0.0 copy-done.2
  6.9 0.0 copy-done.3
  6.9 0.0 copy-done.4
  6.9 0.0 copy-done.5
  6.9 0.0 copy-done.6
  6.9 0.0 copy-done.7
  7.0 0.0 copy-done.8
  7.0 0.0 copy-done.9
  7.0 0.0 copy-done.12
  7.0 65.8 %shard_map.157 = (f32[64,2048]{1,0:T(8,128)S(1)}, f32[64,256]{1,0:T(8,128)S(1)}, f32[64,512]{1,0:T(8,128)S(1)}, f32[64,512]{1,0:T(8,128)S(1)}) custom-call(s32[1,8]{1,0:T(1,128)S(1)} %copy-done.12, bf16[4,2048,256]{2,1,0:T(8,128)(2,1)S(1)} %shard_map.156.dense_ref, f32[1,2048]{1,0:T(1,128)S(1)} %bitcast.6, f32[1,2048]{1,0:T(1,128)S(1)} %bitcast.7, ...), custom_call_target="tpu_custom_call" | custom-call | tf_op jit(solution)/shard_map/pallas_call | solution.py:422
  72.8 0.9 %shard_map.158 = (f32[64,2048]{1,0:T(8,128)}, f32[64,256]{1,0:T(8,128)}, f32[64,512]{1,0:T(8,128)}, f32[64,512]{1,0:T(8,128)}) custom-call(f32[64,2048]{1,0:T(8,128)S(1)} %get-tuple-element.8.refs_0_, f32[64,256]{1,0:T(8,128)S(1)} %get-tuple-element.9.refs_1_, f32[64,512]{1,0:T(8,128)S(1)} %get-tuple-element.10.refs_2_, f32[64,512]{1,0:T(8,128)S(1)} %get-tuple-element.11.refs_3_), custom_call_target="tpu_custom_call" | custom-call | tf_op jit(solution)/shard_map/pallas_call | solution.py:388
  (5 shorter events, 0.0 us)
Async XLA Ops:
  0.6 2.2 %copy-start = (bf16[128,128,128]{2,1,0:T(8,128)(2,1)S(1)}, bf16[128,128,128]{2,1,0:T(8,128)(2,1)}, u32[]{:S(2)}) copy-start(bf16[128,128,128]{2,1,0:T(8,128)(2,1)} %tiles_ref.1) | copy-start | bytes 12582916
  2.8 0.7 copy-start.10
  3.5 0.7 copy-start.11
  4.1 2.8 %copy-start.1 = (f32[512,512]{1,0:T(8,128)S(1)}, f32[512,512]{1,0:T(8,128)}, u32[]{:S(2)}) copy-start(f32[512,512]{1,0:T(8,128)} %whit_ref.1) | copy-start | bytes 3145732
  4.1 2.8 %copy-start.2 = (f32[256,512]{1,0:T(8,128)S(1)}, f32[256,512]{1,0:T(8,128)}, u32[]{:S(2)}) copy-start(f32[256,512]{1,0:T(8,128)} %cov_ref.1) | copy-start | bytes 1572868
  4.1 2.8 %copy-start.3 = (s32[64,256]{1,0:T(8,128)S(1)}, s32[64,256]{1,0:T(8,128)}, u32[]{:S(2)}) copy-start(s32[64,256]{1,0:T(8,128)} %signs_ref.1) | copy-start | bytes 196612
  4.1 2.8 %copy-start.4 = (f32[2048]{0:T(1024)S(1)}, f32[2048]{0:T(1024)}, u32[]{:S(2)}) copy-start(f32[2048]{0:T(1024)} %param.17) | copy-start | bytes 24580
  4.1 2.8 %copy-start.5 = (f32[2048]{0:T(1024)S(1)}, f32[2048]{0:T(1024)}, u32[]{:S(2)}) copy-start(f32[2048]{0:T(1024)} %param.18) | copy-start | bytes 24580
  4.2 2.8 %copy-start.6 = (s32[2048]{0:T(1024)S(1)}, s32[2048]{0:T(1024)}, u32[]{:S(2)}) copy-start(s32[2048]{0:T(1024)} %param.19) | copy-start | bytes 24580
  4.2 2.8 %copy-start.7 = (f32[256]{0:T(256)S(1)}, f32[256]{0:T(256)}, u32[]{:S(2)}) copy-start(f32[256]{0:T(256)} %param.20) | copy-start | bytes 3076
  4.2 2.8 %copy-start.8 = (f32[256]{0:T(256)S(1)}, f32[256]{0:T(256)}, u32[]{:S(2)}) copy-start(f32[256]{0:T(256)} %param.21) | copy-start | bytes 3076
  4.2 2.8 %copy-start.9 = (s32[256]{0:T(256)S(1)}, s32[256]{0:T(256)}, u32[]{:S(2)}) copy-start(s32[256]{0:T(256)} %param.22) | copy-start | bytes 3076
  4.2 2.8 %copy-start.12 = (s32[1,8]{1,0:T(1,128)S(1)}, s32[1,8]{1,0:T(1,128)}, u32[]{:S(2)}) copy-start(s32[1,8]{1,0:T(1,128)} %blocks_ref.1) | copy-start | bytes 100
